TPU v7x, 512 devices: a whole 4x4x16 slice. The times are simulated.
512 devices in a mesh: grp: 64 (over x, z), dev: 8 (over y, core).
Axes of the slice: x: 4, y: 4, z: 16, core: 2. Of those that a mesh axis runs over, the one named last changes fastest.
Arguments:
- tokens: bfloat16 [32768, 768], P(('grp', 'dev')), may hold values from -6 to 6
- expert_ids: int32 [32768, 8], P(('grp', 'dev')), may hold values from 0 to 511, as said below
- gates: bfloat16 [32768, 8], P(('grp', 'dev')), may hold values from 0.099609375 to 0.5
- w_in: bfloat16 [512, 768, 1536], P(('grp', 'dev')), may hold values from -0.21875 to 0.21875
- w_out: bfloat16 [512, 1536, 768], P(('grp', 'dev')), may hold values from -0.15625 to 0.15625
Outputs:
- mixed: bfloat16 [32768, 768], P(('grp', 'dev'))
Inputs may be any that keep to these rules, and one draw needn't show every extreme that they name: `expert_ids`: row t lists 8 experts; columns 2 * k and 2 * k + 1 are two different experts of one group (experts g * 8 to g * 8 + 7 form group g), and the four groups of a row differ. The owner of token t is t // 64, and its dev index is the owner modulo 8. The tokens of one owner pick one group at most 12 times, and every owner reaches it for some group. The tokens whose owners share a dev index pick each group exactly 4 * 64 times in all and each expert at most 192 times; in every group one expert is picked 192 times by the tokens of every dev index.
All inputs are finite; a program needn't handle non-finite values.
Results may differ from a plain program's by a relative error of at most 0.0057.
Values may be sent and summed in bfloat16 or wider, within the bound.
A program may use at most 64 MiB of HBM per device.

v0:
```python
import jax
import jax.numpy as jnp
from jax import lax
from jax.sharding import PartitionSpec as P

F32 = jnp.float32
BF16 = jnp.bfloat16
NX = 4
NZ = 16


def per_device(tokens, expert_ids, gates, w_in, w_out):
    n_dev = lax.axis_size("dev")
    count, width = tokens.shape
    cap = 4 * count
    z_sets = [[x * NZ + z for z in range(NZ)] for x in range(NX)]
    x_sets = [[x * NZ + z for x in range(NX)] for z in range(NZ)]
    me = lax.axis_index("grp")
    my_x, my_z = (me // NZ, me % NZ)
    mine = lax.axis_index("dev")
    pairs = expert_ids.reshape(count, 4, 2)
    gate_pairs = gates.reshape(count, 4, 2)
    meta = jnp.concatenate(
        [
            (pairs[:, :, 0] // n_dev).astype(BF16),
            (pairs[:, :, 0] % n_dev).astype(BF16),
            (pairs[:, :, 1] % n_dev).astype(BF16),
            gate_pairs[:, :, 0],
            gate_pairs[:, :, 1],
        ],
        axis=1,
    ).T
    column = lax.all_gather(tokens, "grp", axis_index_groups=z_sets, tiled=True)
    metas = lax.all_gather(meta, "grp")
    group = metas[:, 0:4, :].astype(jnp.int32)
    tri = (jnp.arange(count)[:, None] < jnp.arange(count)[None, :]).astype(BF16)
    owners = NX * NZ
    tri_o = (jnp.arange(owners)[:, None] < jnp.arange(owners)[None, :]).astype(F32)
    targets = jnp.arange(NX) * NZ + my_z
    match = (group[None] == targets[:, None, None, None]).astype(BF16)
    hit = jnp.sum(match, axis=2)
    within = jnp.dot(hit, tri, preferred_element_type=F32)
    totals = jnp.sum(hit.astype(F32), axis=2)
    base = jnp.dot(totals, tri_o, precision=lax.Precision.HIGHEST)
    place = jnp.where(hit > 0, within + base[:, :, None], -1.0).astype(jnp.int32)
    own = lax.dynamic_slice_in_dim(place, my_x * NZ, NZ, axis=1).reshape(NX, NZ * count)
    rows = jnp.arange(cap)
    select = (own[:, None, :] == rows[None, :, None]).astype(BF16).reshape(NX * cap, NZ * count)
    spread = jnp.dot(select, column, preferred_element_type=F32).astype(BF16)
    group_rows = lax.psum_scatter(
        spread, "grp", scatter_dimension=0, axis_index_groups=x_sets, tiled=True
    )
    all_rows = lax.all_gather(group_rows, "dev", tiled=True)
    place_me = lax.dynamic_index_in_dim(place, my_x, 0, keepdims=False).reshape(-1)
    match_me = lax.dynamic_index_in_dim(match, my_x, 0, keepdims=False)
    facts = jnp.stack(
        [jnp.sum(match_me * metas[:, 4 * i : 4 * i + 4, :], axis=1) for i in range(1, 5)], axis=-1
    ).reshape(owners * count, 4)
    seat = (place_me[None, :] == rows[:, None]).astype(BF16)
    row_facts = jnp.dot(seat, facts, preferred_element_type=F32).astype(BF16)
    all_facts = lax.all_gather(row_facts, "dev", tiled=True)
    who = mine.astype(BF16)
    weight = jnp.where(all_facts[:, 0] == who, all_facts[:, 2], 0).astype(F32) + jnp.where(
        all_facts[:, 1] == who, all_facts[:, 3], 0
    ).astype(F32)
    hidden = jnp.maximum(jnp.dot(all_rows, w_in[0], preferred_element_type=F32), 0.0).astype(BF16)
    out = jnp.dot(hidden, w_out[0], preferred_element_type=F32)
    out = (out * weight[:, None]).astype(BF16)
    group_sum = lax.psum_scatter(out, "dev", scatter_dimension=0, tiled=True)
    back = lax.all_gather(group_sum, "grp", axis_index_groups=x_sets, tiled=True)
    partial_sum = lax.dot_general(
        select, back, (((0,), (0,)), ((), ())), preferred_element_type=F32
    ).astype(BF16)
    return lax.psum_scatter(
        partial_sum, "grp", scatter_dimension=0, axis_index_groups=z_sets, tiled=True
    )


def solution(mesh):
    tok = P(("grp", "dev"), None)
    return jax.shard_map(
        per_device,
        mesh=mesh,
        in_specs=(tok, tok, tok, P(("grp", "dev"), None, None), P(("grp", "dev"), None, None)),
        out_specs=tok,
        check_vma=False,
    )
```

profile of v0, /device:TPU:4, one launch (start us, length us, event | category | flops | bytes accessed | tf_op | source)
XLA Modules:
  0.0 360.3 jit_solution(1277123264415232062)
XLA Ops:
  6.5 0.7 all-gather.6.cloned.1.call-update
  7.4 0.8 fusion.32
  8.1 0.8 fusion.31
  9.0 99.7 %all-gather.1 = bf16[64,20,64]{2,1,0:T(8,128)(2,1)S(1)} all-gather(bf16[1,20,64]{2,1,0:T(8,128)(2,1)S(1)} %bitcast.41), channel_id=2, replica_groups=mesh['grp'=64,'dev'=8] {'grp'}, dimensions={0}, use_global_device_ids=true | all-gather | bytes 166400 | tf_op jit(solution)/shard_map/all_gather | solution.py:34
  108.8 0.5 fusion.30
  109.2 0.1 convert_reduce_fusion
  109.3 0.1 fusion.18
  109.5 0.2 fusion.5
  109.8 1.6 bitcast_compare_fusion
  111.4 4.7 %convolution_convert_fusion.1 = bf16[1024,768]{1,0:T(8,128)(2,1)} fusion(pred[1024,1024]{1,0:T(32,128)(4,1)} %bitcast_compare_fusion, bf16[1024,768]{1,0:T(8,128)(2,1)} %all-gather.6.cloned.1.call-done), kind=kOutput, calls=%fused_computation.9 | convolution fusion | flops 1611399168 | bytes 4194304 | tf_op jit(solution)/shard_map/dot_general | solution.py:49
  116.2 29.0 %reduce-scatter.4.cloned.1.call-done = bf16[256,768]{1,0:T(8,128)(2,1)} async-done(((bf16[1024,768]{1,0:T(8,128)(2,1)}), bf16[256,768]{1,0:T(8,128)(2,1)}) %reduce-scatter.4.cloned.1.call-update) | async-done | bytes 393232 | tf_op jit(solution)/shard_map/reduce_scatter | solution.py:50
  145.3 0.2 compare_convert_fusion
  145.5 0.4 fusion.10
  145.9 0.1 stack.15
  146.1 0.1 stack.16
  146.3 0.8 fusion.6
  147.1 12.0 %all_gather.22 = bf16[2048,4]{0,1:T(4,128)(2,1)S(1)} all-gather(bf16[256,4]{0,1:T(4,128)(2,1)S(1)} %fusion.6), channel_id=1, replica_groups=mesh['grp'=64,'dev'=8] {'dev'}, dimensions={0}, use_global_device_ids=true | all-gather | bytes 18432 | tf_op jit(solution)/shard_map/all_gather | solution.py:61
  159.1 25.1 %all-gather.8.cloned.1.call-done = bf16[2048,768]{1,0:T(8,128)(2,1)} async-done(((bf16[256,768]{1,0:T(8,128)(2,1)}), bf16[2048,768]{1,0:T(8,128)(2,1)}) %all-gather.8.cloned.1.call-update) | async-done | bytes 3145744 | tf_op jit(solution)/shard_map/all_gather | solution.py:53
  184.1 7.3 %maximum_convert_fusion = bf16[2048,1536]{1,0:T(8,128)(2,1)S(1)} fusion(bf16[2048,768]{1,0:T(8,128)(2,1)} %all-gather.8.cloned.1.call-done, bf16[1,768,1536]{2,1,0:T(8,128)(2,1)S(1)} %copy-done), kind=kOutput, calls=%fused_computation | convolution fusion | flops 4838129664 | bytes 11796480 | tf_op jit(solution)/shard_map/dot_general | solution.py:66
  191.5 6.4 %multiply_convert_fusion = bf16[2048,768]{1,0:T(8,128)(2,1)} fusion(bf16[2048,1536]{1,0:T(8,128)(2,1)S(1)} %maximum_convert_fusion, f32[2048]{0:T(1024)S(1)} %bitcast.46, bf16[1,1536,768]{2,1,0:T(8,128)(2,1)S(1)} %copy-done.2), kind=kOutput, calls=%fused_computation.1 | convolution fusion | flops 4834983936 | bytes 11804672 | tf_op jit(solution)/shard_map/dot_general | solution.py:67
  197.9 43.6 %reduce-scatter.6.cloned.1.call-done = bf16[256,768]{1,0:T(8,128)(2,1)} async-done(((bf16[2048,768]{1,0:T(8,128)(2,1)}), bf16[256,768]{1,0:T(8,128)(2,1)}) %reduce-scatter.6.cloned.1.call-update) | async-done | bytes 393232 | tf_op jit(solution)/shard_map/reduce_scatter | solution.py:69
  241.6 33.7 %all-gather.10.cloned.1.call-done = bf16[1024,768]{1,0:T(8,128)(2,1)} async-done(((bf16[256,768]{1,0:T(8,128)(2,1)}), bf16[1024,768]{1,0:T(8,128)(2,1)}) %all-gather.10.cloned.1.call-update) | async-done | bytes 1572880 | tf_op jit(solution)/shard_map/all_gather | solution.py:70
  275.3 4.8 %convolution_convert_fusion = bf16[1024,768]{1,0:T(8,128)(2,1)} fusion(pred[1024,1024]{1,0:T(32,128)(4,1)S(1)} %copy-done.1, bf16[1024,768]{1,0:T(8,128)(2,1)} %all-gather.10.cloned.1.call-done), kind=kOutput, calls=%fused_computation.8 | convolution fusion | flops 1611399168 | bytes 4194304 | tf_op jit(solution)/shard_map/dot_general | solution.py:71
  280.2 73.3 %reduce-scatter.8.cloned.1.call-done = bf16[64,768]{1,0:T(8,128)(2,1)} async-done(((bf16[1024,768]{1,0:T(8,128)(2,1)}), bf16[64,768]{1,0:T(8,128)(2,1)}) %reduce-scatter.8.cloned.1.call-update) | async-done | bytes 98320 | tf_op jit(solution)/shard_map/reduce_scatter | solution.py:74
  (32 shorter events, 0.8 us)
Async XLA Ops:
  6.5 177.6 %copy-start = (bf16[1,768,1536]{2,1,0:T(8,128)(2,1)S(1)}, bf16[1,768,1536]{2,1,0:T(8,128)(2,1)}, u32[]{:S(2)}) copy-start(bf16[1,768,1536]{2,1,0:T(8,128)(2,1)} %param.8) | copy-start | bytes 7077892
  6.5 104.9 %all-gather.6.cloned.1.call-start = ((), (), s32[]{:S(2)}) async-start(), calls=%async_computation.3 | async-start | bytes 1671168 | tf_op jit(solution)/shard_map/all_gather | solution.py:33
  7.3 137.9 %reduce-scatter.4.cloned.1.call-start = ((), (), s32[]{:S(2)}) async-start(), calls=%async_computation.4 | async-start | bytes 1966080 | tf_op jit(solution)/shard_map/reduce_scatter | solution.py:50
  116.1 68.0 %all-gather.8.cloned.1.call-start = ((), (), s32[]{:S(2)}) async-start(), calls=%async_computation.5 | async-start | bytes 3538944 | tf_op jit(solution)/shard_map/all_gather | solution.py:53
  145.1 96.4 %reduce-scatter.6.cloned.1.call-start = ((), (), s32[]{:S(2)}) async-start(), calls=%async_computation.6 | async-start | bytes 3538944 | tf_op jit(solution)/shard_map/reduce_scatter | solution.py:69
  184.1 7.3 %copy-start.2 = (bf16[1,1536,768]{2,1,0:T(8,128)(2,1)S(1)}, bf16[1,1536,768]{2,1,0:T(8,128)(2,1)}, u32[]{:S(2)}) copy-start(bf16[1,1536,768]{2,1,0:T(8,128)(2,1)} %param.9) | copy-start | bytes 7077892
  197.9 77.5 %copy-start.1 = (pred[1024,1024]{1,0:T(32,128)(4,1)S(1)}, pred[1024,1024]{1,0:T(32,128)(4,1)}, u32[]{:S(2)}) copy-start(pred[1024,1024]{1,0:T(32,128)(4,1)} %bitcast_compare_fusion) | copy-start | bytes 3145732
  197.9 77.5 %all-gather.10.cloned.1.call-start = ((), (), s32[]{:S(2)}) async-start(), calls=%async_computation.7 | async-start | bytes 1966080 | tf_op jit(solution)/shard_map/all_gather | solution.py:70
  241.6 111.9 %reduce-scatter.8.cloned.1.call-start = ((), (), s32[]{:S(2)}) async-start(), calls=%async_computation.8 | async-start | bytes 1671168 | tf_op jit(solution)/shard_map/reduce_scatter | solution.py:74
Sparse Core Ops, SparseCore 0:
  9.4 76.8 all-gather.5
  116.2 28.8 reduce-scatter.3
  147.2 36.8 all-gather.7
  198.0 43.4 reduce-scatter.5
  243.5 31.8 all-gather.9
  280.3 73.1 reduce-scatter.7
where the time goes:
time: 360 us
  waiting for transfers between devices  205 us (57%)
  blocking collectives  112 us (31%)
  matrix products  24.3 us (7%)
  between operations  13.6 us (4%)
    all_gather x1, blocking collectives, per_device(): metas = lax.all_gather(meta, 'grp')  99.7 us
    reduce_scatter x1, waiting for transfers between devices, per_device(): lax.psum_scatter(partial_sum, 'grp', scatter_dimension=0, axis_index_grou...  73.3 us
    reduce_scatter x1, waiting for transfers between devices, per_device(): group_sum = lax.psum_scatter(out, 'dev', scatter_dimension=0, tiled=True)  43.6 us
    all_gather x1, waiting for transfers between devices, per_device(): lax.all_gather(group_sum, 'grp', axis_index_groups=x_sets, tiled=True)  33.7 us
    reduce_scatter x1, waiting for transfers between devices, per_device(): lax.psum_scatter(spread, 'grp', scatter_dimension=0, axis_index_groups=x_...  29 us
    all_gather x1, waiting for transfers between devices, per_device(): all_rows = lax.all_gather(group_rows, 'dev', tiled=True)  25.1 us
    all_gather x1, blocking collectives, per_device(): all_facts = lax.all_gather(row_facts, 'dev', tiled=True)  12 us
    dot_general x1, matrix products, per_device(): jnp.dot(all_rows, w_in[0], preferred_element_type=F32)  7.32 us
  transfers between devices with their start and end apart: 6, of which 5 were waited for; matrix products, arithmetic and copies ran while one was open for 2% of the time, Pallas kernels for 0%

commit v1 on v0

--- a/solution.py
+++ b/solution.py
@@ -50,7 +50,15 @@
     group_rows = lax.psum_scatter(
         spread, "grp", scatter_dimension=0, axis_index_groups=x_sets, tiled=True
     )
-    all_rows = lax.all_gather(group_rows, "dev", tiled=True)
+    all_rows = jnp.concatenate(
+        lax.all_to_all(
+            jnp.stack([group_rows for _ in range(lax.axis_size("dev"))]),
+            "dev",
+            split_axis=0,
+            concat_axis=0,
+        ),
+        axis=0,
+    )
     place_me = lax.dynamic_index_in_dim(place, my_x, 0, keepdims=False).reshape(-1)
     match_me = lax.dynamic_index_in_dim(match, my_x, 0, keepdims=False)
     facts = jnp.stack(

time: 360 us -> 372 us (1.033)
  the two profiles are of different devices: /device:TPU:4 before, /device:TPU:6 now
where the time goes in v1:
time: 372 us
  waiting for transfers between devices  181 us (49%)
  blocking collectives  140 us (38%)
  matrix products  24.3 us (7%)
  between operations  13.3 us (4%)
  local copies, waits for them, and re-layouts  5.04 us (1%)
  starting transfers between devices  4.6 us (1%)
    all_gather x1, blocking collectives, per_device(): metas = lax.all_gather(meta, 'grp')  99.5 us
    reduce_scatter x1, waiting for transfers between devices, per_device(): lax.psum_scatter(partial_sum, 'grp', scatter_dimension=0, axis_index_grou...  73.3 us
    reduce_scatter x1, waiting for transfers between devices, per_device(): group_sum = lax.psum_scatter(out, 'dev', scatter_dimension=0, tiled=True)  43.4 us
    all_gather x1, blocking collectives, per_device(): all_facts = lax.all_gather(row_facts, 'dev', tiled=True)  41 us
    all_gather x1, waiting for transfers between devices, per_device(): lax.all_gather(group_sum, 'grp', axis_index_groups=x_sets, tiled=True)  33.9 us
    reduce_scatter x1, waiting for transfers between devices, per_device(): lax.psum_scatter(spread, 'grp', scatter_dimension=0, axis_index_groups=x_...  29.9 us
  transfers between devices with their start and end apart: 6, of which 4 were waited for; matrix products, arithmetic and copies ran while one was open for 2% of the time, Pallas kernels for 0%

profile of v1, /device:TPU:6, one launch (start us, length us, event | category | flops | bytes accessed | tf_op | source)
XLA Modules:
  0.0 371.9 jit_solution(7004375505737287326)
XLA Ops:
  6.5 0.7 all-gather.5.cloned.1.call-update
  7.4 0.8 fusion.32
  8.1 0.8 fusion.31
  9.0 99.5 %all-gather.1 = bf16[64,20,64]{2,1,0:T(8,128)(2,1)S(1)} all-gather(bf16[1,20,64]{2,1,0:T(8,128)(2,1)S(1)} %bitcast.42), channel_id=2, replica_groups=mesh['grp'=64,'dev'=8] {'grp'}, dimensions={0}, use_global_device_ids=true | all-gather | bytes 166400 | tf_op jit(solution)/shard_map/all_gather | solution.py:34
  108.5 0.5 fusion.30
  109.0 0.1 convert_reduce_fusion
  109.1 0.1 fusion.18
  109.2 0.2 fusion.5
  109.5 1.7 bitcast_compare_fusion
  111.2 4.7 %convolution_convert_fusion.1 = bf16[1024,768]{1,0:T(8,128)(2,1)} fusion(pred[1024,1024]{1,0:T(32,128)(4,1)} %bitcast_compare_fusion, bf16[1024,768]{1,0:T(8,128)(2,1)} %all-gather.5.cloned.1.call-done), kind=kOutput, calls=%fused_computation.9 | convolution fusion | flops 1611399168 | bytes 4194304 | tf_op jit(solution)/shard_map/dot_general | solution.py:49
  115.9 29.9 %reduce-scatter.4.cloned.1.call-done = bf16[256,768]{1,0:T(8,128)(2,1)} async-done(((bf16[1024,768]{1,0:T(8,128)(2,1)}), bf16[256,768]{1,0:T(8,128)(2,1)}) %reduce-scatter.4.cloned.1.call-update) | async-done | bytes 393232 | tf_op jit(solution)/shard_map/reduce_scatter | solution.py:50
  145.8 2.9 stack.12
  148.6 4.4 %all-to-all-start = ((bf16[8,256,768]{2,1,0:T(8,128)(2,1)}), bf16[8,256,768]{2,1,0:T(8,128)(2,1)}, u32[]{:S(2)}, u32[]{:S(2)}) async-start(bf16[8,256,768]{2,1,0:T(8,128)(2,1)} %stack.12), calls=%async_computation.1 | async-start | bytes 6291456 | tf_op jit(solution)/shard_map/all_to_all | solution.py:54
  153.2 0.2 compare_convert_fusion
  153.4 0.4 fusion.10
  153.8 0.1 stack.13
  154.2 0.8 fusion.6
  155.0 41.0 %all_gather.18 = bf16[2048,4]{0,1:T(4,128)(2,1)S(1)} all-gather(bf16[256,4]{0,1:T(4,128)(2,1)S(1)} %fusion.6), channel_id=1, replica_groups=mesh['grp'=64,'dev'=8] {'dev'}, dimensions={0}, use_global_device_ids=true | all-gather | bytes 18432 | tf_op jit(solution)/shard_map/all_gather | solution.py:69
  196.1 7.3 %maximum_convert_fusion = bf16[2048,1536]{1,0:T(8,128)(2,1)S(1)} fusion(bf16[2048,768]{1,0:T(8,128)(2,1)} %bitcast.9, bf16[1,768,1536]{2,1,0:T(8,128)(2,1)S(1)} %copy-done), kind=kOutput, calls=%fused_computation | convolution fusion | flops 4838129664 | bytes 11796480 | tf_op jit(solution)/shard_map/dot_general | solution.py:74
  203.5 6.4 %multiply_convert_fusion = bf16[2048,768]{1,0:T(8,128)(2,1)} fusion(bf16[2048,1536]{1,0:T(8,128)(2,1)S(1)} %maximum_convert_fusion, f32[2048]{0:T(1024)S(1)} %bitcast.47, bf16[1,1536,768]{2,1,0:T(8,128)(2,1)S(1)} %copy-done.2), kind=kOutput, calls=%fused_computation.1 | convolution fusion | flops 4834983936 | bytes 11804672 | tf_op jit(solution)/shard_map/dot_general | solution.py:75
  209.9 43.4 %reduce-scatter.6.cloned.1.call-done = bf16[256,768]{1,0:T(8,128)(2,1)} async-done(((bf16[2048,768]{1,0:T(8,128)(2,1)}), bf16[256,768]{1,0:T(8,128)(2,1)}) %reduce-scatter.6.cloned.1.call-update) | async-done | bytes 393232 | tf_op jit(solution)/shard_map/reduce_scatter | solution.py:77
  253.4 33.9 %all-gather.7.cloned.1.call-done = bf16[1024,768]{1,0:T(8,128)(2,1)} async-done(((bf16[256,768]{1,0:T(8,128)(2,1)}), bf16[1024,768]{1,0:T(8,128)(2,1)}) %all-gather.7.cloned.1.call-update) | async-done | bytes 1572880 | tf_op jit(solution)/shard_map/all_gather | solution.py:78
  287.3 4.8 %convolution_convert_fusion = bf16[1024,768]{1,0:T(8,128)(2,1)} fusion(pred[1024,1024]{1,0:T(32,128)(4,1)S(1)} %copy-done.1, bf16[1024,768]{1,0:T(8,128)(2,1)} %all-gather.7.cloned.1.call-done), kind=kOutput, calls=%fused_computation.8 | convolution fusion | flops 1611399168 | bytes 4194304 | tf_op jit(solution)/shard_map/dot_general | solution.py:79
  292.1 73.3 %reduce-scatter.8.cloned.1.call-done = bf16[64,768]{1,0:T(8,128)(2,1)} async-done(((bf16[1024,768]{1,0:T(8,128)(2,1)}), bf16[64,768]{1,0:T(8,128)(2,1)}) %reduce-scatter.8.cloned.1.call-update) | async-done | bytes 98320 | tf_op jit(solution)/shard_map/reduce_scatter | solution.py:82
  (32 shorter events, 0.9 us)
Async XLA Ops:
  6.5 189.6 %copy-start = (bf16[1,768,1536]{2,1,0:T(8,128)(2,1)S(1)}, bf16[1,768,1536]{2,1,0:T(8,128)(2,1)}, u32[]{:S(2)}) copy-start(bf16[1,768,1536]{2,1,0:T(8,128)(2,1)} %param.8) | copy-start | bytes 7077892
  6.5 104.6 %all-gather.5.cloned.1.call-start = ((), (), s32[]{:S(2)}) async-start(), calls=%async_computation.4 | async-start | bytes 1671168 | tf_op jit(solution)/shard_map/all_gather | solution.py:33
  7.3 138.5 %reduce-scatter.4.cloned.1.call-start = ((), (), s32[]{:S(2)}) async-start(), calls=%async_computation.5 | async-start | bytes 1966080 | tf_op jit(solution)/shard_map/reduce_scatter | solution.py:50
  148.6 47.4 %all-to-all-start = ((bf16[8,256,768]{2,1,0:T(8,128)(2,1)}), bf16[8,256,768]{2,1,0:T(8,128)(2,1)}, u32[]{:S(2)}, u32[]{:S(2)}) async-start(bf16[8,256,768]{2,1,0:T(8,128)(2,1)} %stack.12), calls=%async_computation.1 | async-start | bytes 6291456 | tf_op jit(solution)/shard_map/all_to_all | solution.py:54
  153.1 100.2 %reduce-scatter.6.cloned.1.call-start = ((), (), s32[]{:S(2)}) async-start(), calls=%async_computation.6 | async-start | bytes 3538944 | tf_op jit(solution)/shard_map/reduce_scatter | solution.py:77
  196.1 7.4 %copy-start.2 = (bf16[1,1536,768]{2,1,0:T(8,128)(2,1)S(1)}, bf16[1,1536,768]{2,1,0:T(8,128)(2,1)}, u32[]{:S(2)}) copy-start(bf16[1,1536,768]{2,1,0:T(8,128)(2,1)} %param.9) | copy-start | bytes 7077892
  209.8 77.5 %copy-start.1 = (pred[1024,1024]{1,0:T(32,128)(4,1)S(1)}, pred[1024,1024]{1,0:T(32,128)(4,1)}, u32[]{:S(2)}) copy-start(pred[1024,1024]{1,0:T(32,128)(4,1)} %bitcast_compare_fusion) | copy-start | bytes 3145732
  209.9 77.5 %all-gather.7.cloned.1.call-start = ((), (), s32[]{:S(2)}) async-start(), calls=%async_computation.7 | async-start | bytes 1966080 | tf_op jit(solution)/shard_map/all_gather | solution.py:78
  253.3 112.1 %reduce-scatter.8.cloned.1.call-start = ((), (), s32[]{:S(2)}) async-start(), calls=%async_computation.8 | async-start | bytes 1671168 | tf_op jit(solution)/shard_map/reduce_scatter | solution.py:82
Sparse Core Ops, SparseCore 0:
  9.4 77.0 all-gather.4
  116.0 29.7 reduce-scatter.3
  210.0 43.2 reduce-scatter.5
  255.3 31.9 all-gather.6
  292.3 73.1 reduce-scatter.7
